TPU v7x, 512 devices: a whole 4x8x8 slice. The times are simulated.
512 devices in a mesh: grp: 16 (over x_lo, y), dom: 32 (over x_hi, z, core).
Axes of the slice: x: 4 (x_hi: 2, x_lo: 2; x = x_hi * 2 + x_lo), y: 8, z: 8, core: 2. Of those that a mesh axis runs over, the one named last changes fastest.
Arguments:
- pair_blocks: bfloat16 [16, 4096, 3, 4096], P('grp', 'dom'), may hold values from -3 to 3
- pair_target: int32 [16, 4096], P('grp', 'dom'), may hold values from 0 to 31, as said below
- ghost_source: int32 [16, 32, 2, 8], P('grp', 'dom'), may hold values from 0 to 15, as said below
- weight_code: int32 [16, 512], P('grp', 'dom'), may hold values from 0 to 3
- ref_forces: float32 [16, 512, 3], P('grp', 'dom'), may hold values from -6 to 6
Outputs:
- gram: float32 [4096, 4096], P('grp', 'dom')
- rhs: float32 [4096], P('dom')
Inputs may be any that keep to these rules, and one draw needn't show every extreme that they name: `pair_target`: A pair's neighbour slot is never its centre atom. `ghost_source`: entries are distinct within each snapshot, domain and side.
All inputs are finite; a program needn't handle non-finite values.
Results may differ from a plain program's by a relative error of at most 0.0041.
Values may be sent and summed in bfloat16 or wider, within the bound.
A program may use at most 64 MiB of HBM per device.

v0:
```python
import math

import jax
import jax.numpy as jnp
from jax import lax
from jax.sharding import PartitionSpec as P


def from_behind(shard, axis, by):
    devices = lax.axis_size(axis)
    return lax.ppermute(shard, axis, [(i, (i + by) % devices) for i in range(devices)])


def per_device(pair_blocks, pair_target, ghost_source, weight_code, ref_forces):
    pair_count = pair_blocks.shape[1]
    basis_count = pair_blocks.shape[3]
    atom_count = weight_code.shape[1]
    ghosts = ghost_source.shape[3]
    slot_count = atom_count + 2 * ghosts
    per_atom = pair_count // atom_count
    blocks = pair_blocks[0].reshape(pair_count, 3 * basis_count)
    center = jnp.arange(pair_count) // per_atom
    target = pair_target[0]
    slot_ids = jnp.arange(slot_count)[:, None]
    sign_matrix = (slot_ids == center[None, :]).astype(jnp.float32) - (
        slot_ids == target[None, :]
    ).astype(jnp.float32)
    slot_rows = jnp.dot(
        sign_matrix.astype(jnp.bfloat16), blocks, preferred_element_type=jnp.float32
    )
    lower_rows = slot_rows[atom_count : atom_count + ghosts]
    upper_rows = slot_rows[atom_count + ghosts :]
    from_upper = from_behind(lower_rows, "dom", -1)
    from_lower = from_behind(upper_rows, "dom", 1)
    sources = ghost_source[0, 0]
    atom_ids = jnp.arange(atom_count)[None, :]
    onehot_upper = (sources[0][:, None] == atom_ids).astype(jnp.float32)
    onehot_lower = (sources[1][:, None] == atom_ids).astype(jnp.float32)
    owned_rows = slot_rows[:atom_count]
    owned_rows = owned_rows + jnp.dot(onehot_upper.T, from_upper, precision=lax.Precision.HIGHEST)
    owned_rows = owned_rows + jnp.dot(onehot_lower.T, from_lower, precision=lax.Precision.HIGHEST)
    row_scale = (1.0 + weight_code[0].astype(jnp.float32)) * 0.5
    design = (owned_rows.reshape(atom_count, 3, basis_count) * row_scale[:, None, None]).astype(
        jnp.bfloat16
    )
    design = design.reshape(atom_count * 3, basis_count)
    targets = (ref_forces[0] * row_scale[:, None]).astype(jnp.bfloat16).reshape(atom_count * 3, 1)
    dom_count = lax.axis_size("dom")
    grp_count = lax.axis_size("grp")
    factor = 1.0 / math.sqrt(3 * atom_count * dom_count * grp_count)
    contract = (((0,), (0,)), ((), ()))
    panel_rows, panel_targets = (
        lax.all_gather(design, "dom", axis=0, tiled=True),
        lax.all_gather(targets, "dom", axis=0, tiled=True),
    )
    block_width = basis_count // dom_count
    column_block = lax.dynamic_slice_in_dim(
        panel_rows, lax.axis_index("dom") * block_width, block_width, 1
    )
    partial_value = lax.dot_general(
        panel_rows, column_block, contract, preferred_element_type=jnp.float32
    )
    rhs_part = lax.dot_general(
        column_block, panel_targets, contract, preferred_element_type=jnp.float32
    )
    gram_tile = lax.psum_scatter(partial_value, "grp", scatter_dimension=0, tiled=True)
    rhs_tile = lax.psum(rhs_part, "grp").reshape(block_width)
    return (gram_tile * factor, rhs_tile * factor)


def solution(mesh):
    return jax.shard_map(
        per_device,
        mesh=mesh,
        in_specs=(
            P("grp", "dom", None, None),
            P("grp", "dom"),
            P("grp", "dom", None, None),
            P("grp", "dom"),
            P("grp", "dom", None),
        ),
        out_specs=(P("grp", "dom"), P("dom")),
        check_vma=False,
    )
```

profile of v0, /device:TPU:6, one launch (start us, length us, event | category | flops | bytes accessed | tf_op | source)
XLA Modules:
  0.0 282.8 jit_solution(8303352523992524999)
XLA Ops:
  7.2 0.0 all-gather.2.cloned.1.call-start
  7.2 0.0 copy-start.3
  7.2 3.5 %copy.8 = bf16[1,128,3,4096]{1,3,2,0:T(8,128)(2,1)S(1)} copy(bf16[1,128,3,4096]{3,1,2,0:T(8,128)(2,1)} %param.5) | data formatting | bytes 6291456 | tf_op args[0]
  10.7 0.0 copy-done.3
  10.7 0.0 copy-start.4
  10.7 0.0 copy-start.2
  10.8 1.2 fusion.4
  11.9 0.0 copy-start
  11.9 1.2 copy-done
  13.1 0.1 fusion.12
  13.1 11.2 %collective-permute-start = (f32[8,12288]{1,0:T(8,128)S(1)}, f32[8,12288]{1,0:T(8,128)S(1)}, u32[]{:S(2)}, u32[]{:S(2)}) collective-permute-start(f32[8,12288]{1,0:T(8,128)S(1)} %get-tuple-element.2), channel_id=1, source_target_pairs={{0,31},{1,0},{2,1},{3,2},{4,3},{5,4},{6,5},{7,6},{8,7},{9,8},{10,9... | collective-permute-start | bytes 1179656 | tf_op jit(solution)/shard_map/ppermute | solution.py:11
  24.4 1.9 collective-permute-start.1
  26.3 0.0 copy-done.4
  26.3 0.1 mul.62
  26.4 0.1 mul.63
  26.5 0.0 copy-done.2
  26.5 10.6 %collective-permute-done.1 = f32[8,12288]{1,0:T(8,128)S(1)} collective-permute-done((f32[8,12288]{1,0:T(8,128)S(1)}, f32[8,12288]{1,0:T(8,128)S(1)}, u32[]{:S(2)}, u32[]{:S(2)}) %collective-permute-start.1) | collective-permute-done | bytes 393248 | tf_op jit(solution)/shard_map/ppermute | solution.py:11
  37.1 0.6 fusion.7
  37.7 0.0 collective-permute-done
  37.7 1.8 fusion
  39.5 0.2 reshape.78
  39.7 0.9 multiply_convert_fusion
  40.5 0.0 all-gather.2.cloned.1.call-update
  40.6 0.0 reduce-scatter.2.cloned.1.call-start
  40.6 0.0 copy-start.1
  40.6 117.8 %all-gather.2.cloned.1.call-done = bf16[1536,4096]{1,0:T(8,128)(2,1)} async-done(((bf16[48,4096]{1,0:T(8,128)(2,1)}), bf16[1536,4096]{1,0:T(8,128)(2,1)}) %all-gather.2.cloned.1.call-update) | async-done | bytes 12582928 | tf_op jit(solution)/shard_map/all_gather | solution.py:53
  158.5 9.4 %fusion.2 = f32[4096,128]{1,0:T(8,128)} fusion(bf16[1536,4096]{1,0:T(8,128)(2,1)} %all-gather.2.cloned.1.call-done, s32[]{:T(128)S(6)} %select_n.13), kind=kOutput, calls=%fused_computation.5 | convolution fusion | flops 1610612736 | bytes 15073284 | tf_op jit(solution)/shard_map/dot_general | solution.py:60
  167.9 0.0 reduce-scatter.2.cloned.1.call-update
  167.9 0.1 mul.69
  168.0 0.0 copy-done.1
  168.0 0.1 copy.9
  168.1 0.1 squeeze.2
  168.2 1.3 dynamic-slice
  170.1 0.2 dynamic-update-slice
  170.4 68.4 %all-reduce = bf16[1536]{0:T(1024)(128)(2,1)S(1)} all-reduce(bf16[1536]{0:T(1024)(128)(2,1)S(1)} %dynamic-update-slice), channel_id=1, replica_groups=mesh['grp'=16,'dom'=32] {'dom'}, use_global_device_ids=true, to_apply=%add | all-reduce | flops 1536 | bytes 6144 | tf_op jit(solution)/shard_map/reshape.8
  238.7 1.2 convolution_bitcast_fusion
  239.9 33.9 %psum.7 = f32[128,1]{0,1:T(1,128)S(1)} all-reduce(f32[128,1]{0,1:T(1,128)S(1)} %convolution_bitcast_fusion), channel_id=1, replica_groups=mesh['grp'=16,'dom'=32] {'grp'}, use_global_device_ids=true, to_apply=%region_1.2 | all-reduce | flops 128 | bytes 1024 | tf_op jit(solution)/shard_map/psum | solution.py:67
  273.8 0.5 multiply_bitcast_fusion
  274.3 0.0 reduce-scatter.2.cloned.1.call-done
  274.3 1.6 broadcast_multiply_fusion
  (6 shorter events, 0.0 us)
Async XLA Ops:
  7.2 151.3 %all-gather.2.cloned.1.call-start = ((), (), s32[]{:S(2)}) async-start(), calls=%async_computation.1 | async-start | bytes 12976128 | tf_op jit(solution)/shard_map/all_gather | solution.py:53
  7.2 3.5 %copy-start.3 = (s32[1,128]{1,0:T(1,128)S(1)}, s32[1,128]{1,0:T(1,128)}, u32[]{:S(2)}) copy-start(s32[1,128]{1,0:T(1,128)} %param.6) | copy-start | bytes 1540
  10.7 15.6 %copy-start.4 = (s32[1,16]{1,0:T(1,128)S(1)}, s32[1,16]{1,0:T(1,128)}, u32[]{:S(2)}) copy-start(s32[1,16]{1,0:T(1,128)} %param.8) | copy-start | bytes 196
  10.7 15.8 %copy-start.2 = (s32[1,1,2,8]{3,2,1,0:T(2,128)S(1)}, s32[1,1,2,8]{3,2,1,0:T(2,128)}, u32[]{:S(2)}) copy-start(s32[1,1,2,8]{3,2,1,0:T(2,128)} %param.7) | copy-start | bytes 196
  11.9 1.2 copy-start
  13.1 24.5 %collective-permute-start = (f32[8,12288]{1,0:T(8,128)S(1)}, f32[8,12288]{1,0:T(8,128)S(1)}, u32[]{:S(2)}, u32[]{:S(2)}) collective-permute-start(f32[8,12288]{1,0:T(8,128)S(1)} %get-tuple-element.2), channel_id=1, source_target_pairs={{0,31},{1,0},{2,1},{3,2},{4,3},{5,4},{6,5},{7,6},{8,7},{9,8},{10,9... | collective-permute-start | bytes 1179656 | tf_op jit(solution)/shard_map/ppermute | solution.py:11
  24.4 12.7 %collective-permute-start.1 = (f32[8,12288]{1,0:T(8,128)S(1)}, f32[8,12288]{1,0:T(8,128)S(1)}, u32[]{:S(2)}, u32[]{:S(2)}) collective-permute-start(f32[8,12288]{1,0:T(8,128)S(1)} %get-tuple-element.3), channel_id=1, source_target_pairs={{0,1},{1,2},{2,3},{3,4},{4,5},{5,6},{6,7},{7,8},{8,9},{9,10},{10,1... | collective-permute-start | bytes 1179656 | tf_op jit(solution)/shard_map/ppermute | solution.py:11
  40.6 233.8 %reduce-scatter.2.cloned.1.call-start = ((), (), s32[]{:S(2)}) async-start(), calls=%async_computation.2 | async-start | bytes 2228224 | tf_op jit(solution)/shard_map/reduce_scatter | solution.py:66
  40.6 127.4 %copy-start.1 = (f32[1,16,3]{1,0,2:T(1,128)S(1)}, f32[1,16,3]{1,0,2:T(1,128)}, u32[]{:S(2)}) copy-start(f32[1,16,3]{1,0,2:T(1,128)} %param.9) | copy-start | bytes 580
Sparse Core Ops, SparseCore 0:
  40.7 117.7 all-gather.1
  168.0 74.1 reduce-scatter.1
where the time goes:
time: 283 us
  waiting for transfers between devices  128 us (45%)
  blocking collectives  102 us (36%)
  between operations  14.9 us (5%)
  matrix products  14.1 us (5%)
  starting transfers between devices  13.2 us (5%)
  local copies, waits for them, and re-layouts  6.85 us (2%)
  other arithmetic  2.98 us (1%)
    all_gather x1, waiting for transfers between devices, per_device(): lax.all_gather(design, 'dom', axis=0, tiled=True)  118 us
    another operation x1, blocking collectives  68.4 us
    psum x1, blocking collectives, per_device(): rhs_tile = lax.psum(rhs_part, 'grp').reshape(block_width)  33.9 us
    ppermute x2, starting transfers between devices, from_behind(): lax.ppermute(shard, axis, [(i, (i + by) % devices) for i in range(devices)])  13.1 us
    ppermute x2, waiting for transfers between devices, from_behind(): lax.ppermute(shard, axis, [(i, (i + by) % devices) for i in range(devices)])  10.6 us
    dot_general x1, matrix products, per_device(): lax.dot_general(panel_rows, column_block, contract, preferred_element_typ...  9.39 us
    unnamed x15, local copies, waits for them, and re-layouts  6.28 us
  transfers between devices with their start and end apart: 4, of which 2 were waited for; matrix products, arithmetic and copies ran while one was open for 1% of the time, Pallas kernels for 0%

commit v1 on v0

v1 whole, which is shorter than its diff:
```python
import functools
import math

import jax
import jax.numpy as jnp
from jax import lax
from jax.experimental import pallas as pl
from jax.experimental.pallas import tpu as pltpu
from jax.sharding import PartitionSpec as P

MESH = pl.DeviceIdType.MESH
RING = 8
XS = 4
BLOCKS = 5
CHUNKS = 4
F32 = jnp.float32
BF16 = jnp.bfloat16


def chain_lengths(k):
    return (4, 3) if k % 2 == 0 else (3, 4)


def kernel(
    blocks,
    target_ref,
    ghost_ref,
    weight_ref,
    force_ref,
    gram_ref,
    rhs_ref,
    pairs,
    own,
    ghost_out,
    ghost_in,
    rows,
    partial,
    ring_out,
    ring_in,
    kept,
    second_out,
    second_in,
    mirror_out,
    mirror_in,
    rhs_part,
    rhs_in_z,
    rhs_mid,
    rhs_in_y,
    load_sem,
    ghost_send,
    ghost_recv,
    x_send,
    x_recv,
    ring_send,
    ring_recv,
    second_send,
    second_recv,
    mirror_send,
    mirror_recv,
    rhs_send,
    rhs_recv,
):
    basis = blocks.shape[2]
    pair_count = blocks.shape[1]
    atoms = weight_ref.shape[1]
    half_basis = basis // 2
    width = basis // CHUNKS
    half_width = width // 2

    g = lax.axis_index("grp")
    d = lax.axis_index("dom")
    xl, y = g // RING, g % RING
    xh, z, core = d // (2 * RING), (d // 2) % RING, d % 2
    x = xh * 2 + xl
    delta = (z - y + RING) % RING

    def device(x_, y_, z_, core_):
        return {
            "grp": (x_ % 2) * RING + y_,
            "dom": (x_ // 2) * (2 * RING) + z_ * 2 + core_,
        }

    sibling = device(x, y, z, 1 - core)
    right = device((x + 1) % XS, y, z, core)
    left = device((x + XS - 1) % XS, y, z, core)
    dom_count = 4 * RING
    below = {"grp": g, "dom": (d + dom_count - 1) % dom_count}
    above = {"grp": g, "dom": (d + 1) % dom_count}
    off_chip = {"grp": g, "dom": (d + dom_count - 1 + 2 * core) % dom_count}
    mirror_x = (x % 2) * 2 + x // 2

    def remote(src, dst, send_sem, recv_sem, to):
        return pltpu.make_async_remote_copy(
            src_ref=src,
            dst_ref=dst,
            send_sem=send_sem,
            recv_sem=recv_sem,
            device_id=to,
            device_id_type=MESH,
        )

    def load(q):
        columns = pl.ds(q * width, width)
        return pltpu.make_async_copy(
            blocks.at[:, :, columns], pairs.at[:, :, columns], load_sem.at[q]
        )

    for q in range(CHUNKS):
        load(q).start()

    barrier = pltpu.get_barrier_semaphore()

    def greet(to):
        pl.semaphore_signal(barrier, inc=1, device_id=to, device_id_type=MESH)

    for to in (sibling, right, left, off_chip):
        greet(to)
    for step in range(1, RING):
        greet(device(x, (y + step) % RING, z, core))
        greet(device(x, y, (z + step) % RING, core))

    @pl.when(delta % 4 != 0)
    def _():
        greet(device(mirror_x, z, y, 0))
        greet(device(mirror_x, z, y, 1))

    slots = 2 * atoms
    per_atom = pair_count // atoms
    slot_ids = lax.broadcasted_iota(jnp.int32, (slots, pair_count), 0)
    pair_ids = lax.broadcasted_iota(jnp.int32, (slots, pair_count), 1)
    center = pair_ids // per_atom
    signs = (
        (slot_ids == center).astype(F32) - (slot_ids == target_ref[...]).astype(F32)
    ).astype(BF16)

    ghosts = atoms // 2
    row_ids = lax.broadcasted_iota(jnp.int32, (2 * atoms, 2 * atoms), 0)
    col_ids = lax.broadcasted_iota(jnp.int32, (2 * atoms, 2 * atoms), 1)
    source = jnp.zeros((2 * atoms, 2 * atoms), jnp.int32)
    for side in range(2):
        for ghost in range(ghosts):
            here = (col_ids // atoms == side) & (col_ids % ghosts == ghost)
            source = jnp.where(here, ghost_ref[side, ghost], source)
    placed = (row_ids % atoms == source) & (
        row_ids // atoms == (col_ids // ghosts) % 2
    )
    placed = placed.astype(F32).astype(BF16)

    diagonal = lax.broadcasted_iota(jnp.int32, (atoms, atoms), 0) == (
        lax.broadcasted_iota(jnp.int32, (atoms, atoms), 1)
    )

    def as_column(row):
        return jnp.sum(jnp.where(diagonal, row, 0.0), axis=1, keepdims=True)

    scale = as_column((1.0 + weight_ref[...].astype(F32)) * 0.5)
    first_lane = lax.broadcasted_iota(jnp.int32, (atoms, 128), 1) == 0
    my_slot = x * 2 + core
    for comp in range(3):
        column = as_column(force_ref[comp]) * scale
        rows[my_slot, comp * atoms : (comp + 1) * atoms, basis:] = jnp.where(
            first_lane, column, 0.0
        ).astype(BF16)

    def ghost_copy(side, q):
        return remote(
            ghost_out.at[q, side],
            ghost_in.at[q, pl.ds(side * 16, 16)],
            ghost_send.at[side, q],
            ghost_recv.at[side, q],
            below if side == 0 else above,
        )

    for q in range(CHUNKS):
        load(q).wait()
        columns = pl.ds(q * width, width)
        ghost_rows = []
        for comp in range(3):
            slot_rows = jnp.dot(signs, pairs[comp, :, columns], preferred_element_type=F32)
            own[comp, :, columns] = slot_rows[:atoms]
            ghost_rows.append(slot_rows[atoms:])
        for side in range(2):
            part = [rows_[side * ghosts : (side + 1) * ghosts] for rows_ in ghost_rows]
            ghost_out[q, side, :, :width] = jnp.concatenate(part[:2], axis=0).astype(BF16)
            ghost_out[q, side, :, width:] = jnp.concatenate(
                [part[2][:, :half_width], part[2][:, half_width:]], axis=0
            ).astype(BF16)
        if q == 0:
            extra = 2 * (delta % 4 != 0).astype(jnp.int32)
            pl.semaphore_wait(barrier, 4 + 2 * (RING - 1) + extra)
        for side in range(2):
            ghost_copy(side, q).start()

    def span(q, part):
        start, stop = q * width, (q + 1) * width
        middle = start + half_width
        if q == CHUNKS - 1:
            stop = stop + 128
        if part == 0:
            stop = middle
        elif part == 1:
            start = middle
        return pl.ds(start, stop - start)

    slot_right = ((x + 1) % XS) * 2
    slot_left = ((x + XS - 1) % XS) * 2
    slot_far = ((x + 2) % XS) * 2

    def x_copy(kind, q):
        slot, part, to = (
            (my_slot, None, sibling),
            (my_slot, None, right),
            (my_slot, None, left),
            (slot_left + core, None, sibling),
            (slot_right + core, None, sibling),
            (slot_left + core, 0, right),
            (slot_right + core, 1, left),
            (slot_far + core, 0, sibling),
            (slot_far + core, 1, sibling),
        )[kind]
        piece = rows.at[slot, :, span(q, part)]
        return remote(piece, piece, x_send.at[kind, q], x_recv.at[kind, q], to)

    for q in range(CHUNKS):
        columns = pl.ds(q * width, width)
        for side in range(2):
            ghost_copy(side, q).wait_recv()
        placed_rows = jnp.dot(placed, ghost_in[q], preferred_element_type=F32)
        for comp in range(3):
            if comp < 2:
                added = placed_rows[comp * atoms : (comp + 1) * atoms, :width]
            else:
                added = jnp.concatenate(
                    [placed_rows[:atoms, width:], placed_rows[atoms:, width:]], axis=1
                )
            rows[my_slot, comp * atoms : (comp + 1) * atoms, columns] = (
                (own[comp, :, columns] + added) * scale
            ).astype(BF16)
        for kind in (1, 2, 0):
            x_copy(kind, q).start()

    for q in range(CHUNKS):
        for kind, relays in ((1, (5, 3)), (2, (6, 4))):
            x_copy(kind, q).wait_recv()
            for relay in relays:
                x_copy(relay, q).start()
    for q in range(CHUNKS):
        for kind, relay in ((5, 7), (6, 8)):
            x_copy(kind, q).wait_recv()
            x_copy(relay, q).start()
    for q in range(CHUNKS):
        for kind in (0, 3, 4, 7, 8):
            x_copy(kind, q).wait_recv()

    contract = (((0,), (0,)), ((), ()))
    depth = rows.shape[0] * rows.shape[1]

    def right_block(c):
        start = pl.multiple_of(xh * half_basis + (2 * c + core) * 128, 128)
        return rows[:, :, pl.ds(start, 128)].reshape(depth, 128)

    target_rows = rows[:, :, basis:].reshape(depth, 128)
    for c in range(RING):
        rhs_part[c] = lax.dot_general(
            target_rows, right_block(c), contract, preferred_element_type=F32
        )[:8]

    def rhs_copy_z(step):
        to_z = (z + step) % RING
        return remote(
            rhs_part.at[to_z],
            rhs_in_z.at[step - 1],
            rhs_send.at[0, step - 1],
            rhs_recv.at[0, step - 1],
            device(x, y, to_z, core),
        )

    for step in range(1, RING):
        rhs_copy_z(step).start()

    def product(r, carry):
        start = pl.multiple_of(xl * half_basis + r * 256, 256)
        left_block = rows[:, :, pl.ds(start, 256)].reshape(depth, 256)
        right_blocks = jnp.concatenate(
            [right_block((r + k) % RING) for k in range(BLOCKS)], axis=1
        )
        tile = lax.dot_general(
            left_block, right_blocks, contract, preferred_element_type=F32
        )
        for k in range(BLOCKS):
            columns = slice(k * 128, (k + 1) * 128)
            partial[0, r, k] = tile[:128, columns]
            partial[1, (r + k) % RING, k] = tile[128:, columns]
        return carry

    lax.fori_loop(0, RING, product, 0)

    def ring_copy(h, way, step, k):
        if step == 0:
            src = ring_out.at[h, way, k]
        else:
            src = ring_in.at[h, way, step - 1, k]
        by = 1 if way == 0 else RING - 1
        if h == 0:
            to = device(x, (y + by) % RING, z, core)
        else:
            to = device(x, y, (z + by) % RING, core)
        return remote(
            src,
            ring_in.at[h, way, step, k],
            ring_send.at[h, way, step, k],
            ring_recv.at[h, way, step, k],
            to,
        )

    for step in range(4):
        for k in range(BLOCKS):
            for h in range(2):
                here = y if h == 0 else z
                for way in range(2):
                    length = chain_lengths(k)[way]
                    if step >= length:
                        continue
                    if way == 0:
                        dest = (here + length - step) % RING
                    else:
                        dest = (here + RING - length + step) % RING
                    term = partial[h, dest, k]
                    if step == 0:
                        ring_out[h, way, k] = term.astype(BF16)
                    else:
                        ring_copy(h, way, step - 1, k).wait_recv()
                        ring_in[h, way, step - 1, k] = (
                            ring_in[h, way, step - 1, k].astype(F32) + term
                        ).astype(BF16)
                    ring_copy(h, way, step, k).start()
        if step == 0:
            total = rhs_part[z]
            for back in range(1, RING):
                rhs_copy_z(back).wait_recv()
                total = total + rhs_in_z[back - 1]
            rhs_mid[...] = total

            def rhs_copy_y(step_):
                return remote(
                    rhs_mid,
                    rhs_in_y.at[step_ - 1],
                    rhs_send.at[1, step_ - 1],
                    rhs_recv.at[1, step_ - 1],
                    device(x, (y + step_) % RING, z, core),
                )

            for step_ in range(1, RING):
                rhs_copy_y(step_).start()

    def second_copy(h, k):
        if h == 0:
            offset = (y + k + RING - z) % RING
            to = device(x, y, (y + k) % RING, core)
        else:
            offset = (z + RING - k + RING - y) % RING
            to = device(x, (z + RING - k) % RING, z, core)
        return remote(
            second_out.at[h, k],
            second_in.at[h, offset],
            second_send.at[h, k],
            second_recv.at[h, offset],
            to,
        )

    for k in range(BLOCKS):
        for h in range(2):
            here = y if h == 0 else z
            total = partial[h, here, k]
            for way in range(2):
                length = chain_lengths(k)[way]
                ring_copy(h, way, length - 1, k).wait_recv()
                total = total + ring_in[h, way, length - 1, k].astype(F32)

            @pl.when(delta == k)
            def _():
                kept[h] = total

            @pl.when(delta != k)
            def _():
                second_out[h, k] = total.astype(BF16)
                second_copy(h, k).start()

    total = rhs_mid[...]
    for step in range(1, RING):
        rhs_copy_y(step).wait_recv()
        total = total + rhs_in_y[step - 1]
    rhs_ref[...] = total[:1]

    def mirror_copy(h):
        return remote(
            mirror_out.at[h],
            mirror_in.at[core],
            mirror_send.at[h],
            mirror_recv.at[core],
            device(mirror_x, z, y, h),
        )

    def second_arrival(h, offset):
        return remote(
            second_out.at[h, 0],
            second_in.at[h, offset],
            second_send.at[h, 0],
            second_recv.at[h, offset],
            sibling,
        )

    @pl.when(delta < BLOCKS)
    def _():
        for h in range(2):
            total = kept[h]
            for offset in range(1, RING):
                second_arrival(h, offset).wait_recv()
                total = total + second_in[h, offset].astype(F32)
            gram_ref[h * 128 : (h + 1) * 128, :] = total
            mirror_out[h] = total.T

            @pl.when((delta > 0) & (delta < 4))
            def _():
                mirror_copy(h).start()

    @pl.when(delta >= BLOCKS)
    def _():
        for sender in range(2):
            remote(
                mirror_out.at[0],
                mirror_in.at[sender],
                mirror_send.at[0],
                mirror_recv.at[sender],
                sibling,
            ).wait_recv()
            gram_ref[sender * 128 : (sender + 1) * 128, :] = mirror_in[sender]

    for q in range(CHUNKS):
        for side in range(2):
            ghost_copy(side, q).wait_send()
        for kind in range(9):
            x_copy(kind, q).wait_send()
    for k in range(BLOCKS):
        for h in range(2):
            for way in range(2):
                for step in range(chain_lengths(k)[way]):
                    ring_copy(h, way, step, k).wait_send()

            @pl.when(delta != k)
            def _():
                second_copy(h, k).wait_send()

    for step in range(1, RING):
        rhs_copy_z(step).wait_send()
        rhs_copy_y(step).wait_send()

    @pl.when((delta > 0) & (delta < 4))
    def _():
        for h in range(2):
            mirror_copy(h).wait_send()


def per_device(pair_blocks, pair_target, ghost_source, weight_code, ref_forces):
    _, pair_count, comps, basis = pair_blocks.shape
    atoms = weight_code.shape[1]
    width = basis // CHUNKS
    dom_count = lax.axis_size("dom")
    grp_count = lax.axis_size("grp")
    factor = 1.0 / math.sqrt(comps * atoms * dom_count * grp_count)
    dma = pltpu.SemaphoreType.DMA
    vmem = pl.BlockSpec(memory_space=pltpu.VMEM)
    gram, rhs = pl.pallas_call(
        kernel,
        out_shape=(
            jax.ShapeDtypeStruct((256, 128), F32),
            jax.ShapeDtypeStruct((1, 128), F32),
        ),
        in_specs=[
            pl.BlockSpec(memory_space=pl.ANY),
            vmem,
            pl.BlockSpec(memory_space=pltpu.SMEM),
            vmem,
            vmem,
        ],
        out_specs=(vmem, vmem),
        scratch_shapes=[
            pltpu.VMEM((comps, pair_count, basis), BF16),
            pltpu.VMEM((comps, atoms, basis), F32),
            pltpu.VMEM((CHUNKS, 2, 16, width * 3 // 2), BF16),
            pltpu.VMEM((CHUNKS, 32, width * 3 // 2), BF16),
            pltpu.VMEM((2 * XS, comps * atoms, basis + 128), BF16),
            pltpu.VMEM((2, RING, BLOCKS, 128, 128), F32),
            pltpu.VMEM((2, 2, BLOCKS, 128, 128), BF16),
            pltpu.VMEM((2, 2, 4, BLOCKS, 128, 128), BF16),
            pltpu.VMEM((2, 128, 128), F32),
            pltpu.VMEM((2, BLOCKS, 128, 128), BF16),
            pltpu.VMEM((2, RING, 128, 128), BF16),
            pltpu.VMEM((2, 128, 128), F32),
            pltpu.VMEM((2, 128, 128), F32),
            pltpu.VMEM((RING, 8, 128), F32),
            pltpu.VMEM((RING - 1, 8, 128), F32),
            pltpu.VMEM((8, 128), F32),
            pltpu.VMEM((RING - 1, 8, 128), F32),
            dma((CHUNKS,)),
            dma((2, CHUNKS)),
            dma((2, CHUNKS)),
            dma((9, CHUNKS)),
            dma((9, CHUNKS)),
            dma((2, 2, 4, BLOCKS)),
            dma((2, 2, 4, BLOCKS)),
            dma((2, BLOCKS)),
            dma((2, RING)),
            dma((2,)),
            dma((2,)),
            dma((2, RING - 1)),
            dma((2, RING - 1)),
        ],
        compiler_params=pltpu.CompilerParams(
            collective_id=0,
            has_side_effects=True,
            vmem_limit_bytes=48 * 1024 * 1024,
        ),
    )(
        jnp.transpose(pair_blocks[0], (1, 0, 2)),
        pair_target,
        ghost_source[0, 0],
        weight_code,
        jnp.transpose(ref_forces, (2, 0, 1)),
    )
    return gram * factor, rhs.reshape(128) * factor


def solution(mesh):
    return jax.shard_map(
        per_device,
        mesh=mesh,
        in_specs=(
            P("grp", "dom", None, None),
            P("grp", "dom"),
            P("grp", "dom", None, None),
            P("grp", "dom"),
            P("grp", "dom", None),
        ),
        out_specs=(P("grp", "dom"), P("dom")),
        check_vma=False,
    )
```

time: 283 us -> 79.5 us (0.28)
  the two profiles are of different devices: /device:TPU:6 before, /device:TPU:11 now
where the time goes in v1:
time: 79.5 us; the launch traced here: 79.2 us
  Pallas kernels  72.9 us (92%)
  local copies, waits for them, and re-layouts  4.55 us (6%)
  other arithmetic  1.18 us (1%)
    pallas_call x1, Pallas kernels, per_device(): pl.pallas_call(kernel, out_shape=(jax.ShapeDtypeStruct((256, 128), F32),...  72.9 us
    unnamed x10, local copies, waits for them, and re-layouts  4.55 us

profile of v1, /device:TPU:11, one launch (start us, length us, event | category | flops | bytes accessed | tf_op | source)
XLA Modules:
  0.0 79.2 jit_solution(11641300362932790277)
XLA Ops:
  0.6 0.0 copy-start
  0.6 1.9 %copy-done = bf16[1,128,3,4096]{3,1,2,0:T(8,128)(2,1)S(1)} copy-done((bf16[1,128,3,4096]{3,1,2,0:T(8,128)(2,1)S(1)}, bf16[1,128,3,4096]{3,1,2,0:T(8,128)(2,1)}, u32[]{:S(2)}) %copy-start) | copy-done | bytes 3145752
  2.5 0.0 copy-start.1
  2.5 0.7 copy-done.1
  3.2 0.0 copy-start.2
  3.2 0.7 copy-done.2
  3.9 0.0 copy-start.3
  3.9 0.7 copy-done.3
  4.5 0.0 copy-start.4
  4.5 0.7 copy-done.4
  5.2 72.9 %shard_map.68 = (f32[256,128]{1,0:T(8,128)S(1)}, f32[1,128]{1,0:T(1,128)S(1)}) custom-call(bf16[3,128,4096]{2,1,0:T(8,128)(2,1)S(1)} %bitcast.7, s32[1,128]{1,0:T(1,128)S(1)} %copy-done.3, s32[2,8]{1,0:T(2,128)S(1)} %bitcast.9, s32[1,16]{1,0:T(1,128)S(1)} %copy-done.4, f32[3,1,16]{2,1,0:T(1,128)S(1)} %bitcast.8), custom_call_target="tpu_custom_call" | custom-call | tf_op jit(solution)/shard_map/pallas_call | solution.py:473
  78.1 0.7 broadcast_multiply_fusion
  78.7 0.5 multiply_bitcast_fusion
Async XLA Ops:
  0.6 1.9 %copy-start = (bf16[1,128,3,4096]{3,1,2,0:T(8,128)(2,1)S(1)}, bf16[1,128,3,4096]{3,1,2,0:T(8,128)(2,1)}, u32[]{:S(2)}) copy-start(bf16[1,128,3,4096]{3,1,2,0:T(8,128)(2,1)} %param.5) | copy-start | bytes 9437188
  2.5 0.7 copy-start.1
  3.2 0.7 copy-start.2
  3.9 0.7 copy-start.3
  4.5 0.7 copy-start.4

commit v2 on v1

--- a/solution.py
+++ b/solution.py
@@ -11,7 +11,8 @@
 MESH = pl.DeviceIdType.MESH
 RING = 8
 XS = 4
-BLOCKS = 5
+OFFSETS = (1, 3, 6, 0, 4)
+BLOCKS = len(OFFSETS)
 CHUNKS = 4
 F32 = jnp.float32
 BF16 = jnp.bfloat16
@@ -23,12 +24,16 @@
 
 def kernel(
     blocks,
+    target_hbm,
+    ghost_hbm,
+    weight_hbm,
+    force_hbm,
+    gram_ref,
+    rhs_ref,
     target_ref,
     ghost_ref,
     weight_ref,
     force_ref,
-    gram_ref,
-    rhs_ref,
     pairs,
     own,
     ghost_out,
@@ -47,6 +52,7 @@
     rhs_mid,
     rhs_in_y,
     load_sem,
+    small_sem,
     ghost_send,
     ghost_recv,
     x_send,
@@ -105,6 +111,19 @@
             blocks.at[:, :, columns], pairs.at[:, :, columns], load_sem.at[q]
         )
 
+    small_loads = [
+        pltpu.make_async_copy(source, place, small_sem.at[i])
+        for i, (source, place) in enumerate(
+            (
+                (target_hbm, target_ref),
+                (ghost_hbm, ghost_ref),
+                (weight_hbm, weight_ref),
+                (force_hbm, force_ref),
+            )
+        )
+    ]
+    for copy in small_loads:
+        copy.start()
     for q in range(CHUNKS):
         load(q).start()
 
@@ -119,10 +138,16 @@
         greet(device(x, (y + step) % RING, z, core))
         greet(device(x, y, (z + step) % RING, core))
 
+    sends_mirror = (delta == OFFSETS[0]) | (delta == OFFSETS[1]) | (delta == OFFSETS[2])
+    takes_mirror = jnp.logical_not(sends_mirror) & (delta % 4 != 0)
+
     @pl.when(delta % 4 != 0)
     def _():
         greet(device(mirror_x, z, y, 0))
         greet(device(mirror_x, z, y, 1))
+
+    for copy in small_loads:
+        copy.wait()
 
     slots = 2 * atoms
     per_atom = pair_count // atoms
@@ -171,7 +196,7 @@
             below if side == 0 else above,
         )
 
-    for q in range(CHUNKS):
+    def slots_of(q):
         load(q).wait()
         columns = pl.ds(q * width, width)
         ghost_rows = []
@@ -221,7 +246,7 @@
         piece = rows.at[slot, :, span(q, part)]
         return remote(piece, piece, x_send.at[kind, q], x_recv.at[kind, q], to)
 
-    for q in range(CHUNKS):
+    def design_of(q):
         columns = pl.ds(q * width, width)
         for side in range(2):
             ghost_copy(side, q).wait_recv()
@@ -239,6 +264,12 @@
         for kind in (1, 2, 0):
             x_copy(kind, q).start()
 
+    slots_of(0)
+    for q in range(1, CHUNKS):
+        slots_of(q)
+        design_of(q - 1)
+    design_of(CHUNKS - 1)
+
     for q in range(CHUNKS):
         for kind, relays in ((1, (5, 3)), (2, (6, 4))):
             x_copy(kind, q).wait_recv()
@@ -259,11 +290,29 @@
         start = pl.multiple_of(xh * half_basis + (2 * c + core) * 128, 128)
         return rows[:, :, pl.ds(start, 128)].reshape(depth, 128)
 
-    target_rows = rows[:, :, basis:].reshape(depth, 128)
-    for c in range(RING):
-        rhs_part[c] = lax.dot_general(
-            target_rows, right_block(c), contract, preferred_element_type=F32
-        )[:8]
+    def left_block(h, r):
+        start = pl.multiple_of(xl * half_basis + (2 * r + h) * 128, 128)
+        return rows[:, :, pl.ds(start, 128)].reshape(depth, 128)
+
+    def product(by):
+        r = (y + by + RING) % RING
+        right_blocks = jnp.concatenate(
+            [right_block((r + offset) % RING) for offset in OFFSETS], axis=1
+        )
+        tile = lax.dot_general(
+            left_block(0, r), right_blocks, contract, preferred_element_type=F32
+        )
+        for k in range(BLOCKS):
+            partial[0, r, k] = tile[:, k * 128 : (k + 1) * 128]
+        c = (z + by + RING) % RING
+        left_blocks = jnp.concatenate(
+            [left_block(1, (c + RING - offset) % RING) for offset in OFFSETS], axis=1
+        )
+        tile = lax.dot_general(
+            left_blocks, right_block(c), contract, preferred_element_type=F32
+        )
+        for k in range(BLOCKS):
+            partial[1, c, k] = tile[k * 128 : (k + 1) * 128]
 
     def rhs_copy_z(step):
         to_z = (z + step) % RING
@@ -275,25 +324,14 @@
             device(x, y, to_z, core),
         )
 
-    for step in range(1, RING):
-        rhs_copy_z(step).start()
-
-    def product(r, carry):
-        start = pl.multiple_of(xl * half_basis + r * 256, 256)
-        left_block = rows[:, :, pl.ds(start, 256)].reshape(depth, 256)
-        right_blocks = jnp.concatenate(
-            [right_block((r + k) % RING) for k in range(BLOCKS)], axis=1
-        )
-        tile = lax.dot_general(
-            left_block, right_blocks, contract, preferred_element_type=F32
-        )
-        for k in range(BLOCKS):
-            columns = slice(k * 128, (k + 1) * 128)
-            partial[0, r, k] = tile[:128, columns]
-            partial[1, (r + k) % RING, k] = tile[128:, columns]
-        return carry
-
-    lax.fori_loop(0, RING, product, 0)
+    def rhs_copy_y(step):
+        return remote(
+            rhs_mid,
+            rhs_in_y.at[step - 1],
+            rhs_send.at[1, step - 1],
+            rhs_recv.at[1, step - 1],
+            device(x, (y + step) % RING, z, core),
+        )
 
     def ring_copy(h, way, step, k):
         if step == 0:
@@ -313,7 +351,9 @@
             to,
         )
 
-    for step in range(4):
+    for step, ahead in enumerate(((4, 3, -3), (2, -2), (1, -1), (0,))):
+        for by in ahead:
+            product(by)
         for k in range(BLOCKS):
             for h in range(2):
                 here = y if h == 0 else z
@@ -335,31 +375,36 @@
                         ).astype(BF16)
                     ring_copy(h, way, step, k).start()
         if step == 0:
+            target_rows = rows[:, :, basis:].reshape(depth, 128)
+            for c in range(RING):
+                rhs_part[c] = lax.dot_general(
+                    target_rows, right_block(c), contract, preferred_element_type=F32
+                )[:8]
+            for to in range(1, RING):
+                rhs_copy_z(to).start()
+            for q in range(CHUNKS):
+                for side in range(2):
+                    ghost_copy(side, q).wait_send()
+                for kind in range(9):
+                    x_copy(kind, q).wait_send()
+        if step == 1:
             total = rhs_part[z]
             for back in range(1, RING):
                 rhs_copy_z(back).wait_recv()
                 total = total + rhs_in_z[back - 1]
             rhs_mid[...] = total
-
-            def rhs_copy_y(step_):
-                return remote(
-                    rhs_mid,
-                    rhs_in_y.at[step_ - 1],
-                    rhs_send.at[1, step_ - 1],
-                    rhs_recv.at[1, step_ - 1],
-                    device(x, (y + step_) % RING, z, core),
-                )
-
-            for step_ in range(1, RING):
-                rhs_copy_y(step_).start()
+            for to in range(1, RING):
+                rhs_copy_y(to).start()
 
     def second_copy(h, k):
         if h == 0:
-            offset = (y + k + RING - z) % RING
-            to = device(x, y, (y + k) % RING, core)
+            to_z = (y + OFFSETS[k]) % RING
+            offset = (to_z + RING - z) % RING
+            to = device(x, y, to_z, core)
         else:
-            offset = (z + RING - k + RING - y) % RING
-            to = device(x, (z + RING - k) % RING, z, core)
+            to_y = (z + RING - OFFSETS[k]) % RING
+            offset = (to_y + RING - y) % RING
+            to = device(x, to_y, z, core)
         return remote(
             second_out.at[h, k],
             second_in.at[h, offset],
@@ -377,11 +422,11 @@
                 ring_copy(h, way, length - 1, k).wait_recv()
                 total = total + ring_in[h, way, length - 1, k].astype(F32)
 
-            @pl.when(delta == k)
+            @pl.when(delta == OFFSETS[k])
             def _():
                 kept[h] = total
 
-            @pl.when(delta != k)
+            @pl.when(delta != OFFSETS[k])
             def _():
                 second_out[h, k] = total.astype(BF16)
                 second_copy(h, k).start()
@@ -410,7 +455,16 @@
             sibling,
         )
 
-    @pl.when(delta < BLOCKS)
+    for k in range(BLOCKS):
+        for h in range(2):
+            for way in range(2):
+                for step in range(chain_lengths(k)[way]):
+                    ring_copy(h, way, step, k).wait_send()
+    for step in range(1, RING):
+        rhs_copy_z(step).wait_send()
+        rhs_copy_y(step).wait_send()
+
+    @pl.when(jnp.logical_not(takes_mirror))
     def _():
         for h in range(2):
             total = kept[h]
@@ -420,11 +474,11 @@
             gram_ref[h * 128 : (h + 1) * 128, :] = total
             mirror_out[h] = total.T
 
-            @pl.when((delta > 0) & (delta < 4))
+            @pl.when(sends_mirror)
             def _():
                 mirror_copy(h).start()
 
-    @pl.when(delta >= BLOCKS)
+    @pl.when(takes_mirror)
     def _():
         for sender in range(2):
             remote(
@@ -436,26 +490,14 @@
             ).wait_recv()
             gram_ref[sender * 128 : (sender + 1) * 128, :] = mirror_in[sender]
 
-    for q in range(CHUNKS):
-        for side in range(2):
-            ghost_copy(side, q).wait_send()
-        for kind in range(9):
-            x_copy(kind, q).wait_send()
     for k in range(BLOCKS):
         for h in range(2):
-            for way in range(2):
-                for step in range(chain_lengths(k)[way]):
-                    ring_copy(h, way, step, k).wait_send()
-
-            @pl.when(delta != k)
+
+            @pl.when(delta != OFFSETS[k])
             def _():
                 second_copy(h, k).wait_send()
 
-    for step in range(1, RING):
-        rhs_copy_z(step).wait_send()
-        rhs_copy_y(step).wait_send()
-
-    @pl.when((delta > 0) & (delta < 4))
+    @pl.when(sends_mirror)
     def _():
         for h in range(2):
             mirror_copy(h).wait_send()
@@ -478,13 +520,14 @@
         ),
         in_specs=[
             pl.BlockSpec(memory_space=pl.ANY),
-            vmem,
-            pl.BlockSpec(memory_space=pltpu.SMEM),
-            vmem,
-            vmem,
-        ],
+        ]
+        * 5,
         out_specs=(vmem, vmem),
         scratch_shapes=[
+            pltpu.VMEM((1, pair_count), jnp.int32),
+            pltpu.SMEM((2, atoms // 2), jnp.int32),
+            pltpu.VMEM((1, atoms), jnp.int32),
+            pltpu.VMEM((comps, 1, atoms), F32),
             pltpu.VMEM((comps, pair_count, basis), BF16),
             pltpu.VMEM((comps, atoms, basis), F32),
             pltpu.VMEM((CHUNKS, 2, 16, width * 3 // 2), BF16),
@@ -503,6 +546,7 @@
             pltpu.VMEM((8, 128), F32),
             pltpu.VMEM((RING - 1, 8, 128), F32),
             dma((CHUNKS,)),
+            dma((4,)),
             dma((2, CHUNKS)),
             dma((2, CHUNKS)),
             dma((9, CHUNKS)),
@@ -519,7 +563,7 @@
         compiler_params=pltpu.CompilerParams(
             collective_id=0,
             has_side_effects=True,
-            vmem_limit_bytes=48 * 1024 * 1024,
+            vmem_limit_bytes=60 * 1024 * 1024,
         ),
     )(
         jnp.transpose(pair_blocks[0], (1, 0, 2)),

time: 79.5 us -> 71.8 us (0.903)
  the two profiles are of different devices: /device:TPU:11 before, /device:TPU:13 now
where the time goes in v2:
time: 71.8 us; the launch traced here: 71.6 us
  Pallas kernels  68.2 us (95%)
  other arithmetic  2.75 us (4%)
    pallas_call x1, Pallas kernels, per_device(): pl.pallas_call(kernel, out_shape=(jax.ShapeDtypeStruct((256, 128), F32),...  68.2 us
    mul x2, other arithmetic, per_device(): return (gram * factor, rhs.reshape(128) * factor)  2.75 us

profile of v2, /device:TPU:13, one launch (start us, length us, event | category | flops | bytes accessed | tf_op | source)
XLA Modules:
  0.0 71.6 jit_solution(8813062604091720663)
XLA Ops:
  0.6 68.2 %shard_map.68 = (f32[256,128]{1,0:T(8,128)}, f32[1,128]{1,0:T(1,128)}) custom-call(bf16[3,128,4096]{2,1,0:T(8,128)(2,1)} %bitcast.7, s32[1,128]{1,0:T(1,128)} %target_hbm.1, s32[2,8]{1,0:T(2,128)} %bitcast.9, s32[1,16]{1,0:T(1,128)} %weight_hbm.1, f32[3,1,16]{2,1,0:T(1,128)} %bitcast.8), custom_call_target="tpu_custom_call" | custom-call | tf_op jit(solution)/shard_map/pallas_call | solution.py:515
  68.9 1.6 %broadcast_multiply_fusion = f32[256,128]{1,0:T(8,128)} fusion(f32[256,128]{1,0:T(8,128)} %get-tuple-element.4), kind=kLoop, calls=%fused_computation | loop fusion | flops 32768 | bytes 262144 | tf_op jit(solution)/shard_map/mul | solution.py:575
  70.4 1.2 %multiply_bitcast_fusion = f32[128]{0:T(128)} fusion(f32[1,128]{1,0:T(1,128)} %get-tuple-element.5), kind=kLoop, calls=%fused_computation.1 | loop fusion | flops 128 | bytes 1024 | tf_op jit(solution)/shard_map/mul | solution.py:575

commit v3 on v2

--- a/solution.py
+++ b/solution.py
@@ -16,6 +16,15 @@
 CHUNKS = 4
 F32 = jnp.float32
 BF16 = jnp.bfloat16
+
+
+ORDER = ((0, 2, 4), (1, 3))
+CHUNKS = 4
+F32 = jnp.float32
+BF16 = jnp.bfloat16
+
+
+GROUPS = ((0, 3, (4, 3)), (3, 2, (3, 4)))
 
 
 def chain_lengths(k):
@@ -57,6 +66,7 @@
     ghost_recv,
     x_send,
     x_recv,
+    sib_recv,
     ring_send,
     ring_recv,
     second_send,
@@ -105,6 +115,12 @@
             device_id_type=MESH,
         )
 
+    def landed(ref, sem):
+        remote(ref, ref, sem, sem, sibling).wait_recv()
+
+    def gone(ref, sem):
+        remote(ref, ref, sem, sem, sibling).wait_send()
+
     def load(q):
         columns = pl.ds(q * width, width)
         return pltpu.make_async_copy(
@@ -132,19 +148,13 @@
     def greet(to):
         pl.semaphore_signal(barrier, inc=1, device_id=to, device_id_type=MESH)
 
-    for to in (sibling, right, left, off_chip):
+    up, down = (device(x, (y + by) % RING, z, core) for by in (1, RING - 1))
+    greeted = (off_chip, sibling, right, left, up, down)
+    for to in greeted:
         greet(to)
-    for step in range(1, RING):
-        greet(device(x, (y + step) % RING, z, core))
-        greet(device(x, y, (z + step) % RING, core))
 
     sends_mirror = (delta == OFFSETS[0]) | (delta == OFFSETS[1]) | (delta == OFFSETS[2])
     takes_mirror = jnp.logical_not(sends_mirror) & (delta % 4 != 0)
-
-    @pl.when(delta % 4 != 0)
-    def _():
-        greet(device(mirror_x, z, y, 0))
-        greet(device(mirror_x, z, y, 1))
 
     for copy in small_loads:
         copy.wait()
@@ -191,8 +201,8 @@
         return remote(
             ghost_out.at[q, side],
             ghost_in.at[q, pl.ds(side * 16, 16)],
-            ghost_send.at[side, q],
-            ghost_recv.at[side, q],
+            ghost_send.at[0],
+            ghost_recv.at[q],
             below if side == 0 else above,
         )
 
@@ -211,8 +221,7 @@
                 [part[2][:, :half_width], part[2][:, half_width:]], axis=0
             ).astype(BF16)
         if q == 0:
-            extra = 2 * (delta % 4 != 0).astype(jnp.int32)
-            pl.semaphore_wait(barrier, 4 + 2 * (RING - 1) + extra)
+            pl.semaphore_wait(barrier, len(greeted))
         for side in range(2):
             ghost_copy(side, q).start()
 
@@ -244,12 +253,15 @@
             (slot_far + core, 1, sibling),
         )[kind]
         piece = rows.at[slot, :, span(q, part)]
-        return remote(piece, piece, x_send.at[kind, q], x_recv.at[kind, q], to)
+        if kind in (1, 2, 5, 6):
+            recv = x_recv.at[(1, 2, 5, 6).index(kind), q]
+        else:
+            recv = sib_recv.at[0]
+        return remote(piece, piece, x_send.at[0], recv, to)
 
     def design_of(q):
         columns = pl.ds(q * width, width)
-        for side in range(2):
-            ghost_copy(side, q).wait_recv()
+        landed(ghost_in.at[q], ghost_recv.at[q])
         placed_rows = jnp.dot(placed, ghost_in[q], preferred_element_type=F32)
         for comp in range(3):
             if comp < 2:
@@ -264,11 +276,10 @@
         for kind in (1, 2, 0):
             x_copy(kind, q).start()
 
-    slots_of(0)
-    for q in range(1, CHUNKS):
+    for q in range(CHUNKS):
         slots_of(q)
-        design_of(q - 1)
-    design_of(CHUNKS - 1)
+    for q in range(CHUNKS):
+        design_of(q)
 
     for q in range(CHUNKS):
         for kind, relays in ((1, (5, 3)), (2, (6, 4))):
@@ -279,9 +290,7 @@
         for kind, relay in ((5, 7), (6, 8)):
             x_copy(kind, q).wait_recv()
             x_copy(relay, q).start()
-    for q in range(CHUNKS):
-        for kind in (0, 3, 4, 7, 8):
-            x_copy(kind, q).wait_recv()
+    landed(rows.at[pl.ds(0, 4)], sib_recv.at[0])
 
     contract = (((0,), (0,)), ((), ()))
     depth = rows.shape[0] * rows.shape[1]
@@ -309,18 +318,18 @@
             [left_block(1, (c + RING - offset) % RING) for offset in OFFSETS], axis=1
         )
         tile = lax.dot_general(
-            left_blocks, right_block(c), contract, preferred_element_type=F32
+            right_block(c), left_blocks, contract, preferred_element_type=F32
         )
         for k in range(BLOCKS):
-            partial[1, c, k] = tile[k * 128 : (k + 1) * 128]
+            partial[1, c, k] = tile[:, k * 128 : (k + 1) * 128]
 
     def rhs_copy_z(step):
         to_z = (z + step) % RING
         return remote(
             rhs_part.at[to_z],
             rhs_in_z.at[step - 1],
-            rhs_send.at[0, step - 1],
-            rhs_recv.at[0, step - 1],
+            rhs_send.at[0],
+            rhs_recv.at[0],
             device(x, y, to_z, core),
         )
 
@@ -328,39 +337,43 @@
         return remote(
             rhs_mid,
             rhs_in_y.at[step - 1],
-            rhs_send.at[1, step - 1],
-            rhs_recv.at[1, step - 1],
+            rhs_send.at[1],
+            rhs_recv.at[1],
             device(x, (y + step) % RING, z, core),
         )
 
+    ring_to = (
+        (device(x, (y + 1) % RING, z, core), device(x, (y + RING - 1) % RING, z, core)),
+        (device(x, y, (z + 1) % RING, core), device(x, y, (z + RING - 1) % RING, core)),
+    )
+
     def ring_copy(h, way, step, k):
-        if step == 0:
-            src = ring_out.at[h, way, k]
-        else:
-            src = ring_in.at[h, way, step - 1, k]
-        by = 1 if way == 0 else RING - 1
-        if h == 0:
-            to = device(x, (y + by) % RING, z, core)
-        else:
-            to = device(x, y, (z + by) % RING, core)
+        src = ring_out.at[h, way, k] if step == 0 else ring_in.at[h, way, step - 1, k]
         return remote(
             src,
             ring_in.at[h, way, step, k],
-            ring_send.at[h, way, step, k],
-            ring_recv.at[h, way, step, k],
-            to,
-        )
-
-    for step, ahead in enumerate(((4, 3, -3), (2, -2), (1, -1), (0,))):
-        for by in ahead:
-            product(by)
-        for k in range(BLOCKS):
-            for h in range(2):
-                here = y if h == 0 else z
-                for way in range(2):
-                    length = chain_lengths(k)[way]
-                    if step >= length:
-                        continue
+            ring_send.at[step],
+            ring_recv.at[way, step, k],
+            ring_to[h][way],
+        )
+
+    def rhs_products(blocks_):
+        target_rows = rows[:, :, basis:].reshape(depth, 128)[:, :16]
+        for c in blocks_:
+            rhs_part[c] = lax.dot_general(
+                target_rows, right_block(c), contract, preferred_element_type=F32
+            )[:8]
+
+    def ring_step(step, group):
+        for k in ORDER[group]:
+            for way in range(2):
+                length = chain_lengths(k)[way]
+                if step >= length:
+                    continue
+                if step > 0:
+                    landed(ring_in.at[:, way, step - 1, k], ring_recv.at[way, step - 1, k])
+                for h in range(2):
+                    here = y if h == 0 else z
                     if way == 0:
                         dest = (here + length - step) % RING
                     else:
@@ -369,33 +382,30 @@
                     if step == 0:
                         ring_out[h, way, k] = term.astype(BF16)
                     else:
-                        ring_copy(h, way, step - 1, k).wait_recv()
                         ring_in[h, way, step - 1, k] = (
                             ring_in[h, way, step - 1, k].astype(F32) + term
                         ).astype(BF16)
                     ring_copy(h, way, step, k).start()
-        if step == 0:
-            target_rows = rows[:, :, basis:].reshape(depth, 128)
-            for c in range(RING):
-                rhs_part[c] = lax.dot_general(
-                    target_rows, right_block(c), contract, preferred_element_type=F32
-                )[:8]
-            for to in range(1, RING):
-                rhs_copy_z(to).start()
-            for q in range(CHUNKS):
-                for side in range(2):
-                    ghost_copy(side, q).wait_send()
-                for kind in range(9):
-                    x_copy(kind, q).wait_send()
-        if step == 1:
-            total = rhs_part[z]
-            for back in range(1, RING):
-                rhs_copy_z(back).wait_recv()
-                total = total + rhs_in_z[back - 1]
-            rhs_mid[...] = total
-            for to in range(1, RING):
-                rhs_copy_y(to).start()
-
+
+    product(4)
+    product(-3)
+    ring_step(0, 0)
+    product(3)
+    ring_step(0, 1)
+    product(-2)
+    ring_step(1, 0)
+    product(2)
+    ring_step(1, 1)
+    product(-1)
+    ring_step(2, 0)
+    product(1)
+    ring_step(2, 1)
+    rhs_products(range(0, RING))
+    product(0)
+    ring_step(3, 0)
+    gone(ghost_out, ghost_send.at[0])
+    gone(rows.at[pl.ds(0, 7)], x_send.at[0])
+    ring_step(3, 1)
     def second_copy(h, k):
         if h == 0:
             to_z = (y + OFFSETS[k]) % RING
@@ -408,19 +418,21 @@
         return remote(
             second_out.at[h, k],
             second_in.at[h, offset],
-            second_send.at[h, k],
-            second_recv.at[h, offset],
+            second_send.at[0],
+            second_recv.at[h],
             to,
         )
 
-    for k in range(BLOCKS):
+    for k in ORDER[0] + ORDER[1]:
+        lengths = chain_lengths(k)
+        for way in range(2):
+            last = lengths[way] - 1
+            landed(ring_in.at[:, way, last, k], ring_recv.at[way, last, k])
         for h in range(2):
             here = y if h == 0 else z
             total = partial[h, here, k]
             for way in range(2):
-                length = chain_lengths(k)[way]
-                ring_copy(h, way, length - 1, k).wait_recv()
-                total = total + ring_in[h, way, length - 1, k].astype(F32)
+                total = total + ring_in[h, way, lengths[way] - 1, k].astype(F32)
 
             @pl.when(delta == OFFSETS[k])
             def _():
@@ -431,76 +443,69 @@
                 second_out[h, k] = total.astype(BF16)
                 second_copy(h, k).start()
 
-    total = rhs_mid[...]
-    for step in range(1, RING):
-        rhs_copy_y(step).wait_recv()
-        total = total + rhs_in_y[step - 1]
-    rhs_ref[...] = total[:1]
+    for to in range(1, RING):
+        rhs_copy_z(to).start()
+
+    for step in range(3):
+        gone(ring_in.at[:, :, step], ring_send.at[step])
+    gone(ring_out.at[0], ring_send.at[3])
 
     def mirror_copy(h):
         return remote(
             mirror_out.at[h],
             mirror_in.at[core],
-            mirror_send.at[h],
-            mirror_recv.at[core],
+            mirror_send.at[0],
+            mirror_recv.at[0],
             device(mirror_x, z, y, h),
         )
-
-    def second_arrival(h, offset):
-        return remote(
-            second_out.at[h, 0],
-            second_in.at[h, offset],
-            second_send.at[h, 0],
-            second_recv.at[h, offset],
-            sibling,
-        )
-
-    for k in range(BLOCKS):
-        for h in range(2):
-            for way in range(2):
-                for step in range(chain_lengths(k)[way]):
-                    ring_copy(h, way, step, k).wait_send()
-    for step in range(1, RING):
-        rhs_copy_z(step).wait_send()
-        rhs_copy_y(step).wait_send()
 
     @pl.when(jnp.logical_not(takes_mirror))
     def _():
         for h in range(2):
             total = kept[h]
+            landed(second_in.at[h, pl.ds(1, RING - 1)], second_recv.at[h])
             for offset in range(1, RING):
-                second_arrival(h, offset).wait_recv()
                 total = total + second_in[h, offset].astype(F32)
-            gram_ref[h * 128 : (h + 1) * 128, :] = total
-            mirror_out[h] = total.T
+            flipped = total.T
+            mirror_out[h] = (flipped if h == 0 else total).astype(BF16)
 
             @pl.when(sends_mirror)
             def _():
                 mirror_copy(h).start()
 
+            gram_ref[h * 128 : (h + 1) * 128, :] = total if h == 0 else flipped
+
+    landed(rhs_in_z, rhs_recv.at[0])
+    total = rhs_part[z]
+    for back in range(1, RING):
+        total = total + rhs_in_z[back - 1]
+    rhs_mid[...] = total
+    for to in range(1, RING):
+        rhs_copy_y(to).start()
+
+    gone(rhs_in_z, rhs_send.at[0])
+
+    @pl.when(jnp.logical_not(takes_mirror))
+    def _():
+        gone(second_out.at[:, pl.ds(0, BLOCKS - 1)], second_send.at[0])
+
     @pl.when(takes_mirror)
     def _():
+        gone(second_out, second_send.at[0])
+        landed(mirror_in, mirror_recv.at[0])
         for sender in range(2):
-            remote(
-                mirror_out.at[0],
-                mirror_in.at[sender],
-                mirror_send.at[0],
-                mirror_recv.at[sender],
-                sibling,
-            ).wait_recv()
-            gram_ref[sender * 128 : (sender + 1) * 128, :] = mirror_in[sender]
-
-    for k in range(BLOCKS):
-        for h in range(2):
-
-            @pl.when(delta != OFFSETS[k])
-            def _():
-                second_copy(h, k).wait_send()
+            gram_ref[sender * 128 : (sender + 1) * 128, :] = mirror_in[sender].astype(F32)
+
+    landed(rhs_in_y, rhs_recv.at[1])
+    total = rhs_mid[...]
+    for back in range(1, RING):
+        total = total + rhs_in_y[back - 1]
+    rhs_ref[...] = total[:1]
+    gone(rhs_in_y, rhs_send.at[1])
 
     @pl.when(sends_mirror)
     def _():
-        for h in range(2):
-            mirror_copy(h).wait_send()
+        gone(mirror_out, mirror_send.at[0])
 
 
 def per_device(pair_blocks, pair_target, ghost_source, weight_code, ref_forces):
@@ -539,26 +544,27 @@
             pltpu.VMEM((2, 128, 128), F32),
             pltpu.VMEM((2, BLOCKS, 128, 128), BF16),
             pltpu.VMEM((2, RING, 128, 128), BF16),
-            pltpu.VMEM((2, 128, 128), F32),
-            pltpu.VMEM((2, 128, 128), F32),
+            pltpu.VMEM((2, 128, 128), BF16),
+            pltpu.VMEM((2, 128, 128), BF16),
             pltpu.VMEM((RING, 8, 128), F32),
             pltpu.VMEM((RING - 1, 8, 128), F32),
             pltpu.VMEM((8, 128), F32),
             pltpu.VMEM((RING - 1, 8, 128), F32),
             dma((CHUNKS,)),
             dma((4,)),
-            dma((2, CHUNKS)),
-            dma((2, CHUNKS)),
-            dma((9, CHUNKS)),
-            dma((9, CHUNKS)),
-            dma((2, 2, 4, BLOCKS)),
-            dma((2, 2, 4, BLOCKS)),
-            dma((2, BLOCKS)),
-            dma((2, RING)),
+            dma((1,)),
+            dma((CHUNKS,)),
+            dma((1,)),
+            dma((4, CHUNKS)),
+            dma((1,)),
+            dma((4,)),
+            dma((2, 4, BLOCKS)),
+            dma((1,)),
+            dma((2,)),
+            dma((1,)),
+            dma((1,)),
             dma((2,)),
             dma((2,)),
-            dma((2, RING - 1)),
-            dma((2, RING - 1)),
         ],
         compiler_params=pltpu.CompilerParams(
             collective_id=0,

time: 71.8 us -> 65.7 us (0.915)
  the two profiles are of different devices: /device:TPU:13 before, /device:TPU:4 now
where the time goes in v3:
time: 65.7 us; the launch traced here: 65.5 us
  Pallas kernels  62.1 us (95%)
  other arithmetic  2.75 us (4%)
    pallas_call x1, Pallas kernels, per_device(): pl.pallas_call(kernel, out_shape=(jax.ShapeDtypeStruct((256, 128), F32),...  62.1 us
    mul x2, other arithmetic, per_device(): return (gram * factor, rhs.reshape(128) * factor)  2.75 us

profile of v3, /device:TPU:4, one launch (start us, length us, event | category | flops | bytes accessed | tf_op | source)
XLA Modules:
  0.0 65.5 jit_solution(1095122218443374667)
XLA Ops:
  0.6 62.1 %shard_map.68 = (f32[256,128]{1,0:T(8,128)}, f32[1,128]{1,0:T(1,128)}) custom-call(bf16[3,128,4096]{2,1,0:T(8,128)(2,1)} %bitcast.7, s32[1,128]{1,0:T(1,128)} %target_hbm.1, s32[2,8]{1,0:T(2,128)} %bitcast.9, s32[1,16]{1,0:T(1,128)} %weight_hbm.1, f32[3,1,16]{2,1,0:T(1,128)} %bitcast.8), custom_call_target="tpu_custom_call" | custom-call | tf_op jit(solution)/shard_map/pallas_call | solution.py:520
  62.8 1.6 %broadcast_multiply_fusion = f32[256,128]{1,0:T(8,128)} fusion(f32[256,128]{1,0:T(8,128)} %get-tuple-element.4), kind=kLoop, calls=%fused_computation | loop fusion | flops 32768 | bytes 262144 | tf_op jit(solution)/shard_map/mul | solution.py:581
  64.3 1.2 %multiply_bitcast_fusion = f32[128]{0:T(128)} fusion(f32[1,128]{1,0:T(1,128)} %get-tuple-element.5), kind=kLoop, calls=%fused_computation.1 | loop fusion | flops 128 | bytes 1024 | tf_op jit(solution)/shard_map/mul | solution.py:581

commit v4 on v3

--- a/solution.py
+++ b/solution.py
@@ -11,20 +11,14 @@
 MESH = pl.DeviceIdType.MESH
 RING = 8
 XS = 4
-OFFSETS = (1, 3, 6, 0, 4)
+OFFSETS = (6, 0, 3, 4, 1)
+MIRRORED = (1, 3, 6)
 BLOCKS = len(OFFSETS)
+ORDER = ((0, 2, 4), (1, 3))
+RHS_HOPS = (4, 3)
 CHUNKS = 4
 F32 = jnp.float32
 BF16 = jnp.bfloat16
-
-
-ORDER = ((0, 2, 4), (1, 3))
-CHUNKS = 4
-F32 = jnp.float32
-BF16 = jnp.bfloat16
-
-
-GROUPS = ((0, 3, (4, 3)), (3, 2, (3, 4)))
 
 
 def chain_lengths(k):
@@ -38,7 +32,6 @@
     weight_hbm,
     force_hbm,
     gram_ref,
-    rhs_ref,
     target_ref,
     ghost_ref,
     weight_ref,
@@ -56,8 +49,8 @@
     second_in,
     mirror_out,
     mirror_in,
-    rhs_part,
-    rhs_in_z,
+    rhs_ring_out,
+    rhs_ring_in,
     rhs_mid,
     rhs_in_y,
     load_sem,
@@ -74,6 +67,7 @@
     mirror_send,
     mirror_recv,
     rhs_send,
+    rhs_ring_recv,
     rhs_recv,
 ):
     basis = blocks.shape[2]
@@ -153,7 +147,7 @@
     for to in greeted:
         greet(to)
 
-    sends_mirror = (delta == OFFSETS[0]) | (delta == OFFSETS[1]) | (delta == OFFSETS[2])
+    sends_mirror = (delta == MIRRORED[0]) | (delta == MIRRORED[1]) | (delta == MIRRORED[2])
     takes_mirror = jnp.logical_not(sends_mirror) & (delta % 4 != 0)
 
     for copy in small_loads:
@@ -323,14 +317,18 @@
         for k in range(BLOCKS):
             partial[1, c, k] = tile[:, k * 128 : (k + 1) * 128]
 
-    def rhs_copy_z(step):
-        to_z = (z + step) % RING
+    ring_to = (
+        (device(x, (y + 1) % RING, z, core), device(x, (y + RING - 1) % RING, z, core)),
+        (device(x, y, (z + 1) % RING, core), device(x, y, (z + RING - 1) % RING, core)),
+    )
+
+    def rhs_copy_z(way, step):
         return remote(
-            rhs_part.at[to_z],
-            rhs_in_z.at[step - 1],
+            rhs_ring_out.at[way] if step == 0 else rhs_ring_in.at[way, step - 1],
+            rhs_ring_in.at[way, step],
             rhs_send.at[0],
-            rhs_recv.at[0],
-            device(x, y, to_z, core),
+            rhs_ring_recv.at[way, step],
+            ring_to[1][way],
         )
 
     def rhs_copy_y(step):
@@ -338,14 +336,9 @@
             rhs_mid,
             rhs_in_y.at[step - 1],
             rhs_send.at[1],
-            rhs_recv.at[1],
+            rhs_recv.at[0],
             device(x, (y + step) % RING, z, core),
         )
-
-    ring_to = (
-        (device(x, (y + 1) % RING, z, core), device(x, (y + RING - 1) % RING, z, core)),
-        (device(x, y, (z + 1) % RING, core), device(x, y, (z + RING - 1) % RING, core)),
-    )
 
     def ring_copy(h, way, step, k):
         src = ring_out.at[h, way, k] if step == 0 else ring_in.at[h, way, step - 1, k]
@@ -357,12 +350,24 @@
             ring_to[h][way],
         )
 
-    def rhs_products(blocks_):
+    def rhs_term(by):
         target_rows = rows[:, :, basis:].reshape(depth, 128)[:, :16]
-        for c in blocks_:
-            rhs_part[c] = lax.dot_general(
-                target_rows, right_block(c), contract, preferred_element_type=F32
-            )[:8]
+        c = (z + by + RING) % RING
+        return lax.dot_general(
+            target_rows, right_block(c), contract, preferred_element_type=F32
+        )[:8]
+
+    def rhs_step(step):
+        for way, length in enumerate(RHS_HOPS):
+            if step >= length:
+                continue
+            term = rhs_term(length - step if way == 0 else step - length)
+            if step == 0:
+                rhs_ring_out[way] = term
+            else:
+                landed(rhs_ring_in.at[way, step - 1], rhs_ring_recv.at[way, step - 1])
+                rhs_ring_in[way, step - 1] = rhs_ring_in[way, step - 1] + term
+            rhs_copy_z(way, step).start()
 
     def ring_step(step, group):
         for k in ORDER[group]:
@@ -396,16 +401,21 @@
     ring_step(1, 0)
     product(2)
     ring_step(1, 1)
+    rhs_step(0)
     product(-1)
     ring_step(2, 0)
     product(1)
+    rhs_step(1)
     ring_step(2, 1)
-    rhs_products(range(0, RING))
     product(0)
-    ring_step(3, 0)
     gone(ghost_out, ghost_send.at[0])
     gone(rows.at[pl.ds(0, 7)], x_send.at[0])
+    rhs_step(2)
+    ring_step(3, 0)
+    rhs_mid[...] = rhs_term(0)
+    rhs_step(3)
     ring_step(3, 1)
+
     def second_copy(h, k):
         if h == 0:
             to_z = (y + OFFSETS[k]) % RING
@@ -418,37 +428,49 @@
         return remote(
             second_out.at[h, k],
             second_in.at[h, offset],
-            second_send.at[0],
+            second_send.at[k % 2],
             second_recv.at[h],
             to,
         )
 
-    for k in ORDER[0] + ORDER[1]:
-        lengths = chain_lengths(k)
-        for way in range(2):
-            last = lengths[way] - 1
-            landed(ring_in.at[:, way, last, k], ring_recv.at[way, last, k])
-        for h in range(2):
-            here = y if h == 0 else z
-            total = partial[h, here, k]
+    def finish(group):
+        for k in ORDER[group]:
+            lengths = chain_lengths(k)
             for way in range(2):
-                total = total + ring_in[h, way, lengths[way] - 1, k].astype(F32)
-
-            @pl.when(delta == OFFSETS[k])
-            def _():
-                kept[h] = total
-
-            @pl.when(delta != OFFSETS[k])
-            def _():
-                second_out[h, k] = total.astype(BF16)
-                second_copy(h, k).start()
-
+                last = lengths[way] - 1
+                landed(ring_in.at[:, way, last, k], ring_recv.at[way, last, k])
+            for h in range(2):
+                here = y if h == 0 else z
+                total = partial[h, here, k]
+                for way in range(2):
+                    total = total + ring_in[h, way, lengths[way] - 1, k].astype(F32)
+
+                @pl.when(delta == OFFSETS[k])
+                def _():
+                    kept[h] = total
+
+                @pl.when(delta != OFFSETS[k])
+                def _():
+                    second_out[h, k] = total.astype(BF16)
+                    second_copy(h, k).start()
+
+
+    finish(0)
+    for way, length in enumerate(RHS_HOPS):
+        landed(rhs_ring_in.at[way, length - 1], rhs_ring_recv.at[way, length - 1])
+        rhs_mid[...] += rhs_ring_in[way, length - 1]
     for to in range(1, RING):
-        rhs_copy_z(to).start()
-
-    for step in range(3):
-        gone(ring_in.at[:, :, step], ring_send.at[step])
-    gone(ring_out.at[0], ring_send.at[3])
+        rhs_copy_y(to).start()
+
+    @pl.when(sends_mirror)
+    def _():
+        gone(second_out.at[:, pl.ds(0, 2)], second_send.at[0])
+
+    @pl.when(jnp.logical_not(sends_mirror))
+    def _():
+        gone(second_out.at[:, pl.ds(0, 3)], second_send.at[0])
+
+    finish(1)
 
     def mirror_copy(h):
         return remote(
@@ -475,32 +497,31 @@
 
             gram_ref[h * 128 : (h + 1) * 128, :] = total if h == 0 else flipped
 
-    landed(rhs_in_z, rhs_recv.at[0])
-    total = rhs_part[z]
-    for back in range(1, RING):
-        total = total + rhs_in_z[back - 1]
-    rhs_mid[...] = total
-    for to in range(1, RING):
-        rhs_copy_y(to).start()
-
-    gone(rhs_in_z, rhs_send.at[0])
-
-    @pl.when(jnp.logical_not(takes_mirror))
+    for step in range(3):
+        gone(ring_in.at[:, :, step], ring_send.at[step])
+    gone(ring_out.at[0], ring_send.at[3])
+
+    gone(rhs_in_y, rhs_send.at[0])
+
+    @pl.when(delta % 4 == 0)
     def _():
-        gone(second_out.at[:, pl.ds(0, BLOCKS - 1)], second_send.at[0])
+        gone(second_out.at[:, pl.ds(0, 1)], second_send.at[1])
+
+    @pl.when(delta % 4 != 0)
+    def _():
+        gone(second_out.at[:, pl.ds(0, 2)], second_send.at[1])
 
     @pl.when(takes_mirror)
     def _():
-        gone(second_out, second_send.at[0])
         landed(mirror_in, mirror_recv.at[0])
         for sender in range(2):
             gram_ref[sender * 128 : (sender + 1) * 128, :] = mirror_in[sender].astype(F32)
 
-    landed(rhs_in_y, rhs_recv.at[1])
+    landed(rhs_in_y, rhs_recv.at[0])
     total = rhs_mid[...]
     for back in range(1, RING):
         total = total + rhs_in_y[back - 1]
-    rhs_ref[...] = total[:1]
+    gram_ref[256:264] = total
     gone(rhs_in_y, rhs_send.at[1])
 
     @pl.when(sends_mirror)
@@ -517,17 +538,16 @@
     factor = 1.0 / math.sqrt(comps * atoms * dom_count * grp_count)
     dma = pltpu.SemaphoreType.DMA
     vmem = pl.BlockSpec(memory_space=pltpu.VMEM)
-    gram, rhs = pl.pallas_call(
+    (both,) = pl.pallas_call(
         kernel,
         out_shape=(
-            jax.ShapeDtypeStruct((256, 128), F32),
-            jax.ShapeDtypeStruct((1, 128), F32),
+            jax.ShapeDtypeStruct((264, 128), F32),
         ),
         in_specs=[
             pl.BlockSpec(memory_space=pl.ANY),
         ]
         * 5,
-        out_specs=(vmem, vmem),
+        out_specs=(vmem,),
         scratch_shapes=[
             pltpu.VMEM((1, pair_count), jnp.int32),
             pltpu.SMEM((2, atoms // 2), jnp.int32),
@@ -546,8 +566,8 @@
             pltpu.VMEM((2, RING, 128, 128), BF16),
             pltpu.VMEM((2, 128, 128), BF16),
             pltpu.VMEM((2, 128, 128), BF16),
-            pltpu.VMEM((RING, 8, 128), F32),
-            pltpu.VMEM((RING - 1, 8, 128), F32),
+            pltpu.VMEM((2, 8, 128), F32),
+            pltpu.VMEM((2, 4, 8, 128), F32),
             pltpu.VMEM((8, 128), F32),
             pltpu.VMEM((RING - 1, 8, 128), F32),
             dma((CHUNKS,)),
@@ -559,12 +579,13 @@
             dma((1,)),
             dma((4,)),
             dma((2, 4, BLOCKS)),
-            dma((1,)),
+            dma((2,)),
             dma((2,)),
             dma((1,)),
             dma((1,)),
             dma((2,)),
-            dma((2,)),
+            dma((2, 4)),
+            dma((1,)),
         ],
         compiler_params=pltpu.CompilerParams(
             collective_id=0,
@@ -578,7 +599,8 @@
         weight_code,
         jnp.transpose(ref_forces, (2, 0, 1)),
     )
-    return gram * factor, rhs.reshape(128) * factor
+    both = both * factor
+    return both[:256], both[256]
 
 
 def solution(mesh):

time: 65.7 us -> 65.6 us (level)
  the two profiles are of different devices: /device:TPU:4 before, /device:TPU:11 now
where the time goes in v4:
time: 65.6 us; the launch traced here: 65.5 us
  Pallas kernels  62.7 us (96%)
  local copies, waits for them, and re-layouts  1.18 us (2%)
  other arithmetic  0.92 us (1%)
    pallas_call x1, Pallas kernels, per_device(): pl.pallas_call(kernel, out_shape=(jax.ShapeDtypeStruct((264, 128), F32),)...  62.7 us

profile of v4, /device:TPU:11, one launch (start us, length us, event | category | flops | bytes accessed | tf_op | source)
XLA Modules:
  0.0 65.5 jit_solution(11159074982452724740)
XLA Ops:
  0.6 62.7 %shard_map.68 = f32[264,128]{1,0:T(8,128)} custom-call(bf16[3,128,4096]{2,1,0:T(8,128)(2,1)} %bitcast.7, s32[1,128]{1,0:T(1,128)} %target_hbm.1, s32[2,8]{1,0:T(2,128)} %bitcast.9, s32[1,16]{1,0:T(1,128)} %weight_hbm.1, f32[3,1,16]{2,1,0:T(1,128)} %bitcast.8), custom_call_target="tpu_custom_call" | custom-call | tf_op jit(solution)/shard_map/pallas_call | solution.py:541
  63.4 0.9 %broadcast_multiply_fusion = f32[264,128]{1,0:T(8,128)S(1)} fusion(f32[264,128]{1,0:T(8,128)} %shard_map.68), kind=kLoop, calls=%fused_computation | loop fusion | flops 33792 | bytes 270336 | tf_op jit(solution)/shard_map/mul | solution.py:602
  64.3 0.5 slice_bitcast_fusion
  64.8 0.7 %slice.8 = f32[256,128]{1,0:T(8,128)} slice(f32[264,128]{1,0:T(8,128)S(1)} %broadcast_multiply_fusion), slice={[0:256], [0:128]} | slice | bytes 262144 | tf_op jit(solution)/shard_map/slice | solution.py:603

commit v5 on v4

--- a/solution.py
+++ b/solution.py
@@ -346,7 +346,7 @@
             src,
             ring_in.at[h, way, step, k],
             ring_send.at[step],
-            ring_recv.at[way, step, k],
+            ring_recv.at[step, k],
             ring_to[h][way],
         )
 
@@ -371,12 +371,12 @@
 
     def ring_step(step, group):
         for k in ORDER[group]:
+            if step > 0:
+                landed(ring_in.at[:, :, step - 1, k], ring_recv.at[step - 1, k])
             for way in range(2):
                 length = chain_lengths(k)[way]
                 if step >= length:
                     continue
-                if step > 0:
-                    landed(ring_in.at[:, way, step - 1, k], ring_recv.at[way, step - 1, k])
                 for h in range(2):
                     here = y if h == 0 else z
                     if way == 0:
@@ -436,9 +436,8 @@
     def finish(group):
         for k in ORDER[group]:
             lengths = chain_lengths(k)
-            for way in range(2):
-                last = lengths[way] - 1
-                landed(ring_in.at[:, way, last, k], ring_recv.at[way, last, k])
+            longer = lengths.index(4)
+            landed(ring_in.at[:, longer, 3, k], ring_recv.at[3, k])
             for h in range(2):
                 here = y if h == 0 else z
                 total = partial[h, here, k]
@@ -578,7 +577,7 @@
             dma((4, CHUNKS)),
             dma((1,)),
             dma((4,)),
-            dma((2, 4, BLOCKS)),
+            dma((4, BLOCKS)),
             dma((2,)),
             dma((2,)),
             dma((1,)),

time: 65.6 us -> 65.2 us (level)
  no operation moved by 1% of the time
where the time goes in v5:
time: 65.2 us; the launch traced here: 65.1 us
  Pallas kernels  62.4 us (96%)
  local copies, waits for them, and re-layouts  1.18 us (2%)
  other arithmetic  0.92 us (1%)
    pallas_call x1, Pallas kernels, per_device(): pl.pallas_call(kernel, out_shape=(jax.ShapeDtypeStruct((264, 128), F32),)...  62.4 us

profile of v5, /device:TPU:11, one launch (start us, length us, event | category | flops | bytes accessed | tf_op | source)
XLA Modules:
  0.0 65.1 jit_solution(9227903452351011891)
XLA Ops:
  0.6 62.4 %shard_map.68 = f32[264,128]{1,0:T(8,128)} custom-call(bf16[3,128,4096]{2,1,0:T(8,128)(2,1)} %bitcast.7, s32[1,128]{1,0:T(1,128)} %target_hbm.1, s32[2,8]{1,0:T(2,128)} %bitcast.9, s32[1,16]{1,0:T(1,128)} %weight_hbm.1, f32[3,1,16]{2,1,0:T(1,128)} %bitcast.8), custom_call_target="tpu_custom_call" | custom-call | tf_op jit(solution)/shard_map/pallas_call | solution.py:540
  63.0 0.9 %broadcast_multiply_fusion = f32[264,128]{1,0:T(8,128)S(1)} fusion(f32[264,128]{1,0:T(8,128)} %shard_map.68), kind=kLoop, calls=%fused_computation | loop fusion | flops 33792 | bytes 270336 | tf_op jit(solution)/shard_map/mul | solution.py:601
  63.9 0.5 slice_bitcast_fusion
  64.4 0.7 %slice.8 = f32[256,128]{1,0:T(8,128)} slice(f32[264,128]{1,0:T(8,128)S(1)} %broadcast_multiply_fusion), slice={[0:256], [0:128]} | slice | bytes 262144 | tf_op jit(solution)/shard_map/slice | solution.py:602

commit v6 on v5

--- a/solution.py
+++ b/solution.py
@@ -397,24 +397,24 @@
     ring_step(0, 0)
     product(3)
     ring_step(0, 1)
+    rhs_step(0)
     product(-2)
     ring_step(1, 0)
     product(2)
     ring_step(1, 1)
-    rhs_step(0)
+    rhs_step(1)
     product(-1)
     ring_step(2, 0)
     product(1)
-    rhs_step(1)
     ring_step(2, 1)
+    rhs_step(2)
     product(0)
     gone(ghost_out, ghost_send.at[0])
     gone(rows.at[pl.ds(0, 7)], x_send.at[0])
-    rhs_step(2)
+    rhs_mid[...] = rhs_term(0)
     ring_step(3, 0)
-    rhs_mid[...] = rhs_term(0)
+    ring_step(3, 1)
     rhs_step(3)
-    ring_step(3, 1)
 
     def second_copy(h, k):
         if h == 0:

time: 65.2 us -> 63.8 us (0.979)
  Pallas kernels: 62.4 us -> 60.9 us
    pallas_call x1, Pallas kernels: 62.4 us -> 60.9 us  [per_device(): pl.pallas_call(kernel, out_shape=(jax.ShapeDtypeStruct((264, 128), F32),)...]
where the time goes in v6:
time: 63.8 us; the launch traced here: 63.6 us
  Pallas kernels  60.9 us (95%)
  local copies, waits for them, and re-layouts  1.18 us (2%)
  other arithmetic  0.92 us (1%)
  between operations  0.64 us (1%)
    pallas_call x1, Pallas kernels, per_device(): pl.pallas_call(kernel, out_shape=(jax.ShapeDtypeStruct((264, 128), F32),)...  60.9 us

profile of v6, /device:TPU:11, one launch (start us, length us, event | category | flops | bytes accessed | tf_op | source)
XLA Modules:
  0.0 63.6 jit_solution(14211727577869158970)
XLA Ops:
  0.6 60.9 %shard_map.68 = f32[264,128]{1,0:T(8,128)} custom-call(bf16[3,128,4096]{2,1,0:T(8,128)(2,1)} %bitcast.7, s32[1,128]{1,0:T(1,128)} %target_hbm.1, s32[2,8]{1,0:T(2,128)} %bitcast.9, s32[1,16]{1,0:T(1,128)} %weight_hbm.1, f32[3,1,16]{2,1,0:T(1,128)} %bitcast.8), custom_call_target="tpu_custom_call" | custom-call | tf_op jit(solution)/shard_map/pallas_call | solution.py:540
  61.5 0.9 %broadcast_multiply_fusion = f32[264,128]{1,0:T(8,128)S(1)} fusion(f32[264,128]{1,0:T(8,128)} %shard_map.68), kind=kLoop, calls=%fused_computation | loop fusion | flops 33792 | bytes 270336 | tf_op jit(solution)/shard_map/mul | solution.py:601
  62.4 0.5 slice_bitcast_fusion
  62.9 0.7 %slice.8 = f32[256,128]{1,0:T(8,128)} slice(f32[264,128]{1,0:T(8,128)S(1)} %broadcast_multiply_fusion), slice={[0:256], [0:128]} | slice | bytes 262144 | tf_op jit(solution)/shard_map/slice | solution.py:602
